TPU v7x, 256 devices: a whole 4x4x8 slice. The times are simulated.
256 devices in a mesh: dp: 4 (over x), fsdp: 64 (over z, y, core).
Axes of the slice: x: 4, y: 4, z: 8, core: 2. Of those that a mesh axis runs over, the one named last changes fastest.
Arguments:
- grad_parts: bfloat16 [4, 144, 1024, 1024], P('dp', None, 'fsdp'), may hold values from -64 to 64
- factors: bfloat16 [4, 64, 1, 2, 1024, 1024], P('dp', 'fsdp'), may hold values from -1 to 6
- weights: bfloat16 [144, 1024, 1024], P('dp', 'fsdp'), may hold values from -0.0625 to 0.0625
- block_owner: int32 [144], replicated, may hold values from 0 to 63, as said below
Outputs:
- recast: bfloat16 [144, 1024, 1024], P('dp', 'fsdp')
Inputs may be any that keep to these rules, and one draw needn't show every extreme that they name: `block_owner`: blocks of group g are g * 36 to (g + 1) * 36 - 1. Within each group no fsdp index owns more than 1 block, and in every group one owns exactly 1.
All inputs are finite; a program needn't handle non-finite values.
Results may differ from a plain program's by a relative error of at most 0.028.
Values may be sent and summed in bfloat16 or wider, within the bound.
A program may use at most 64 MiB of HBM per device.

v0:
```python
import math

import jax
import jax.numpy as jnp
from jax import lax
from jax.sharding import PartitionSpec as P

D = 8192
KVW = 1024
BS = 1024


learn_rate = 0.02
small_eps = 1e-06


def block_products(operands):
    block_grad, factor_pair = operands
    right_product = jnp.dot(block_grad, factor_pair[1], preferred_element_type=jnp.float32).astype(
        jnp.bfloat16
    )
    precond = jnp.dot(factor_pair[0], right_product, preferred_element_type=jnp.float32)
    block_wide = block_grad.astype(jnp.float32)
    return (precond, jnp.sum(block_wide * block_wide), jnp.sum(precond * precond))


def per_device(grad_parts, factors, weights, block_owner):
    fsdp_count = lax.axis_size("fsdp")
    group_blocks, shard_rows, block_size = weights.shape
    slot_count = factors.shape[2]
    summed = lax.psum_scatter(
        grad_parts[0].astype(jnp.float32).astype(jnp.bfloat16),
        "dp",
        scatter_dimension=0,
        tiled=True,
    )
    entries = float(group_blocks * lax.axis_size("dp") * block_size * block_size)
    group_index = lax.axis_index("dp")
    local_ids = jnp.arange(group_blocks, dtype=jnp.int32)
    owners_here = lax.dynamic_slice_in_dim(block_owner, group_index * group_blocks, group_blocks)
    earlier_same = (owners_here[:, None] == owners_here[None, :]) & (
        local_ids[None, :] < local_ids[:, None]
    )
    slot_of = jnp.sum(earlier_same.astype(jnp.int32), axis=1)
    dest_key = owners_here * slot_count + slot_of
    targets = jnp.arange(fsdp_count * slot_count, dtype=jnp.int32)
    chosen = (
        jnp.sum(
            jnp.where(dest_key[None, :] == targets[:, None], local_ids[None, :] - group_blocks, 0),
            axis=1,
        )
        + group_blocks
    )
    query_blocks = D * D // (BS * BS)
    key_blocks = D * KVW // (BS * BS)
    global_block = group_index * group_blocks + local_ids
    tensor_id = (
        (global_block >= query_blocks).astype(jnp.int32)
        + (global_block >= query_blocks + key_blocks).astype(jnp.int32)
        + (global_block >= query_blocks + 2 * key_blocks).astype(jnp.int32)
    )
    tensor_range = jnp.arange(4, dtype=jnp.int32)
    padded = jnp.concatenate([summed, jnp.zeros((1, shard_rows, block_size), summed.dtype)], axis=0)
    outgoing = jnp.take(padded, chosen, axis=0).reshape(
        fsdp_count, slot_count, shard_rows, block_size
    )
    arrived = lax.all_to_all(outgoing, "fsdp", split_axis=0, concat_axis=2, tiled=True)
    held = arrived.reshape(slot_count, block_size, block_size)
    precond, grad_squares, prec_squares = lax.map(block_products, (held, factors[0, 0]))
    squares_sum = lax.psum(jnp.sum(grad_squares), ("dp", "fsdp"))
    global_scale = 0.5 * math.sqrt(entries) / jnp.sqrt(squares_sum)
    count = float(block_size * block_size)
    graft_ratio = jnp.sqrt((grad_squares / count + small_eps) / (prec_squares / count + small_eps))
    update = (global_scale * graft_ratio[:, None, None] * precond).astype(jnp.bfloat16)
    returned = lax.all_to_all(
        update.reshape(slot_count, fsdp_count, shard_rows, block_size),
        "fsdp",
        split_axis=1,
        concat_axis=0,
        tiled=True,
    )
    update_here = jnp.take(
        returned.reshape(fsdp_count * slot_count, shard_rows, block_size), dest_key, axis=0
    )
    new_weight = (
        weights.astype(jnp.float32) - learn_rate * update_here.astype(jnp.float32)
    ).astype(jnp.bfloat16)
    block_peak = jnp.max(jnp.abs(new_weight.astype(jnp.float32)), axis=(1, 2))
    local_peak = jnp.max(
        jnp.where(tensor_id[None, :] == tensor_range[:, None], block_peak[None, :], 0.0), axis=1
    )
    tensor_max = lax.pmax(local_peak, ("dp", "fsdp"))
    block_scale = jnp.sum(
        jnp.where(tensor_id[:, None] == tensor_range[None, :], tensor_max[None, :], 0.0), axis=1
    )
    recast = new_weight.astype(jnp.float32) / (block_scale + small_eps)[:, None, None]
    return recast.astype(jnp.bfloat16)


def solution(mesh):
    placed = (
        P("dp", None, "fsdp", None),
        P("dp", "fsdp", None, None, None, None),
        P("dp", "fsdp", None),
        P(),
    )
    return jax.shard_map(
        per_device, mesh=mesh, in_specs=placed, out_specs=P("dp", "fsdp", None), check_vma=False
    )
```

profile of v0, /device:TPU:1, one launch (start us, length us, event | category | flops | bytes accessed | tf_op | source)
XLA Modules:
  0.0 364.5 jit_solution(7145512752959552692)
XLA Ops:
  6.5 0.0 reduce-scatter.2.cloned.1.call-start
  6.5 0.0 copy-start.1
  6.5 0.7 reduce-scatter.2.cloned.1.call-update
  7.3 0.0 copy-done.1
  7.3 0.1 dynamic_slice.9
  7.4 0.2 convert_reduce_fusion
  7.5 0.1 compare_and_fusion.1
  7.6 0.1 select_reduce_fusion
  7.8 59.7 %reduce-scatter.2.cloned.1.call-done = bf16[36,16,1024]{2,1,0:T(8,128)(2,1)} async-done(((bf16[144,16,1024]{2,1,0:T(8,128)(2,1)}), bf16[36,16,1024]{2,1,0:T(8,128)(2,1)}) %reduce-scatter.2.cloned.1.call-update) | async-done | bytes 1179664 | tf_op jit(solution)/shard_map/reduce_scatter | solution.py:31
  67.4 1.4 concatenate.3
  68.8 0.7 gather_fusion
  69.5 0.3 bitcast_select_fusion
  69.8 60.1 %all_to_all.8 = bf16[64,1,16,1024]{3,2,1,0:T(8,128)(2,1)S(1)} all-to-all(bf16[64,1,16,1024]{3,2,1,0:T(8,128)(2,1)S(1)} %bitcast_select_fusion), channel_id=1, replica_groups=mesh['dp'=4,'fsdp'=64] {'fsdp'}, dimensions={0} | all-to-all | bytes 4194304 | tf_op jit(solution)/shard_map/all_to_all | solution.py:67
  129.9 1.7 multiply_reduce_fusion.1
  131.6 75.1 %psum.7 = f32[]{:T(128)} all-reduce(f32[]{:T(128)} %multiply_reduce_fusion.1), channel_id=1, replica_groups=mesh['dp'=4,'fsdp'=64] {'dp','fsdp'}, use_global_device_ids=true, to_apply=%region_4.5 | all-reduce | flops 1 | bytes 8 | tf_op jit(solution)/shard_map/psum | solution.py:70
  207.4 9.3 %multiply_reduce_fusion = (f32[]{:T(128)}, f32[1024,1024]{0,1:T(8,128)}) fusion(bf16[1024,1024]{1,0:T(8,128)(2,1)S(1)} %bitcast.31, bf16[1,1,1,2,1024,1024]{5,4,3,2,1,0:T(8,128)(2,1)} %param.5), kind=kOutput, calls=%fused_computation.3 | convolution fusion | flops 4298113024 | bytes 10485764 | tf_op jit(solution)/shard_map/while/body/eval_jaxpr/dot_general | solution.py:22
  218.0 4.1 %multiply_convert_fusion = bf16[1024,1024]{0,1:T(8,128)(2,1)} fusion(f32[1024,1024]{0,1:T(8,128)} %get-tuple-element.24, f32[]{:T(128)S(6)} %mul.48), kind=kLoop, calls=%fused_computation.2 | loop fusion | flops 2097152 | bytes 6291460 | tf_op jit(solution)/shard_map/convert_element_type | solution.py:74
  222.1 6.1 %all-to-all-start.1 = ((bf16[1,64,16,1024]{3,2,0,1:T(8,128)(2,1)}), bf16[1,64,16,1024]{3,2,0,1:T(8,128)(2,1)S(1)}, u32[]{:S(2)}, u32[]{:S(2)}) async-start(bf16[1,64,16,1024]{3,2,0,1:T(8,128)(2,1)} %bitcast.10), calls=%async_computation.2 | async-start | bytes 4194304 | tf_op jit(solution)/shard_map/all_to_all | solution.py:75
  228.3 49.6 %all-to-all-done.1 = bf16[1,64,16,1024]{3,2,0,1:T(8,128)(2,1)S(1)} async-done(((bf16[1,64,16,1024]{3,2,0,1:T(8,128)(2,1)}), bf16[1,64,16,1024]{3,2,0,1:T(8,128)(2,1)S(1)}, u32[]{:S(2)}, u32[]{:S(2)}) %all-to-all-start.1) | async-done | bytes 2097184 | tf_op jit(solution)/shard_map/all_to_all | solution.py:75
  277.9 0.6 gather_fusion.1
  278.6 0.0 copy-start
  278.6 2.1 fusion
  280.7 0.1 select_reduce_fusion.2
  280.8 75.2 %pmax.7 = f32[4]{0:T(128)S(1)} all-reduce(f32[4]{0:T(128)S(1)} %select_reduce_fusion.2), channel_id=1, replica_groups=mesh['dp'=4,'fsdp'=64] {'dp','fsdp'}, use_global_device_ids=true, to_apply=%region_8.9 | all-reduce | flops 4 | bytes 32 | tf_op jit(solution)/shard_map/pmax | solution.py:92
  356.0 0.1 select_reduce_fusion.1
  356.1 0.0 copy-done
  356.1 1.6 fusion.1
  (8 shorter events, 0.0 us)
Async XLA Ops:
  6.5 60.9 %reduce-scatter.2.cloned.1.call-start = ((), (), s32[]{:S(2)}) async-start(), calls=%async_computation.3 | async-start | bytes 5898240 | tf_op jit(solution)/shard_map/reduce_scatter | solution.py:31
  6.5 0.7 copy-start.1
  222.1 55.8 %all-to-all-start.1 = ((bf16[1,64,16,1024]{3,2,0,1:T(8,128)(2,1)}), bf16[1,64,16,1024]{3,2,0,1:T(8,128)(2,1)S(1)}, u32[]{:S(2)}, u32[]{:S(2)}) async-start(bf16[1,64,16,1024]{3,2,0,1:T(8,128)(2,1)} %bitcast.10), calls=%async_computation.2 | async-start | bytes 4194304 | tf_op jit(solution)/shard_map/all_to_all | solution.py:75
  278.6 77.5 %copy-start = (bf16[36,16,1024]{2,1,0:T(8,128)(2,1)S(1)}, bf16[36,16,1024]{2,1,0:T(8,128)(2,1)}, u32[]{:S(2)}) copy-start(bf16[36,16,1024]{2,1,0:T(8,128)(2,1)} %param.6) | copy-start | bytes 3538948
Sparse Core Ops, SparseCore 0:
  9.9 57.4 reduce-scatter.1
where the time goes:
time: 365 us
  blocking collectives  210 us (58%)
  waiting for transfers between devices  110 us (30%)
  between operations  15.5 us (4%)
  other arithmetic  10.4 us (3%)
  matrix products  9.27 us (3%)
  starting transfers between devices  6.11 us (2%)
    pmax x1, blocking collectives, per_device(): tensor_max = lax.pmax(local_peak, ('dp', 'fsdp'))  75.2 us
    psum x1, blocking collectives, per_device(): squares_sum = lax.psum(jnp.sum(grad_squares), ('dp', 'fsdp'))  75.1 us
    all_to_all x1, blocking collectives, per_device(): lax.all_to_all(outgoing, 'fsdp', split_axis=0, concat_axis=2, tiled=True)  60.1 us
    reduce_scatter x1, waiting for transfers between devices, per_device(): lax.psum_scatter(grad_parts[0].astype(jnp.float32).astype(jnp.bfloat16),...  59.7 us
    all_to_all x1, waiting for transfers between devices, per_device(): lax.all_to_all(update.reshape(slot_count, fsdp_count, shard_rows, block_s...  49.6 us
    dot_general x1, matrix products, block_products(): jnp.dot(factor_pair[0], right_product, preferred_element_type=jnp.float32)  9.27 us
  transfers between devices with their start and end apart: 2, of which 2 were waited for; matrix products, arithmetic and copies ran while one was open for 0% of the time, Pallas kernels for 0%

commit v1 on v0

v1 whole, which is shorter than its diff:
```python
import functools
import math

import jax
import jax.numpy as jnp
from jax import lax
from jax.experimental import pallas as pl
from jax.experimental.pallas import tpu as pltpu
from jax.sharding import PartitionSpec as P

BS = 1024
GB = 36
HALF = 18
NX, NZ, NY = 4, 8, 8
SLOTS = NZ * NY
ROWS = 16
CH = 4
W = BS // CH
PADB = 40

learn_rate = 0.02
small_eps = 1e-06
f32 = jnp.float32
bf16 = jnp.bfloat16
MESH = pl.DeviceIdType.MESH


def kernel(
    chosen, dkey, ownmat, grads, factors, weights, out,
    gin, fac, win, xa, xs, xb, summed, zsend, zrcv, gbuf, acc, rp, pbuf, yrcv, fin,
    gsq, psq, sc, bmax, sty, stz, stx, mxy, mxz, mxx,
    in_sem, xsnd, xrcv, zsnd, zrs, ysnd, yrs, csnd, crs, dsnd, drs, st_snd, st_rcv,
):
    g = lax.axis_index("dp")
    f = lax.axis_index("fsdp")
    z = lax.div(f, NY)
    yc = lax.rem(f, NY)

    def xdev(d):
        return {"dp": lax.rem(g + d, NX)}

    def zdev(d):
        return {"fsdp": lax.rem(z + d, NZ) * NY + yc}

    def ydev(d):
        return {"fsdp": z * NY + lax.rem(yc + d, NY)}

    loads = [
        pltpu.make_async_copy(grads.at[:, :, pl.ds(k * W, W)], gin.at[k], in_sem.at[k])
        for k in range(CH)
    ]
    load_f = pltpu.make_async_copy(factors, fac, in_sem.at[CH])
    load_w = pltpu.make_async_copy(weights, win, in_sem.at[CH + 1])
    for c in loads:
        c.start()
    load_f.start()
    load_w.start()

    barrier = pltpu.get_barrier_semaphore()
    peers = (
        [xdev(d) for d in range(1, NX)]
        + [zdev(d) for d in range(1, NZ)]
        + [ydev(d) for d in range(1, NY)]
    )
    for p in peers:
        pl.semaphore_signal(barrier, inc=1, device_id=p, device_id_type=MESH)
    gsq[...] = jnp.zeros_like(gsq)
    psq[...] = jnp.zeros_like(psq)
    pl.semaphore_wait(barrier, len(peers))

    sends = []

    def send(src, dst, ss, rs, dev):
        c = pltpu.make_async_remote_copy(
            src_ref=src, dst_ref=dst, send_sem=ss, recv_sem=rs, device_id=dev, device_id_type=MESH
        )
        c.start()
        return c

    gnext = lax.rem(g + 1, NX) * GB
    gprev = lax.rem(g + 3, NX) * GB
    gfar = lax.rem(g + 2, NX) * GB
    gown = g * GB

    def x1(k):
        loads[k].wait()
        a = send(gin.at[k, pl.ds(gfar, HALF)], xa.at[0, k], xsnd.at[0, 0, k], xrcv.at[0, 0, k], xdev(1))
        b = send(gin.at[k, pl.ds(gfar + HALF, HALF)], xa.at[1, k], xsnd.at[0, 1, k], xrcv.at[0, 1, k], xdev(3))
        sends.extend([a, b])
        return a, b

    def x2own(k):
        a = send(
            gin.at[k, pl.ds(gnext + HALF, HALF)], xb.at[0, k, pl.ds(HALF, HALF)],
            xsnd.at[1, 0, k], xrcv.at[1, 0, k], xdev(1),
        )
        b = send(
            gin.at[k, pl.ds(gprev, HALF)], xb.at[1, k, pl.ds(0, HALF)],
            xsnd.at[1, 1, k], xrcv.at[1, 1, k], xdev(3),
        )
        sends.extend([a, b])
        return a, b

    def x2sum(k, first):
        out_c = []
        for side, base in ((0, gnext), (1, gprev + HALF)):
            first[side].wait_recv()

            @pl.loop(0, HALF, unroll=3)
            def _(i):
                xs[side, k, i] = (gin[k, base + i].astype(f32) + xa[side, k, i].astype(f32)).astype(bf16)

            at = pl.ds(0, HALF) if side == 0 else pl.ds(HALF, HALF)
            out_c.append(
                send(
                    xs.at[side, k], xb.at[side, k, at],
                    xsnd.at[2, side, k], xrcv.at[2, side, k], xdev(1 if side == 0 else 3),
                )
            )
        sends.extend(out_c)
        return out_c

    def pack_and_z(k, got):
        for c in got:
            c.wait_recv()

        @pl.loop(0, GB, unroll=4)
        def _(b):
            v = gin[k, gown + b].astype(f32) + xb[0, k, b].astype(f32) + xb[1, k, b].astype(f32)
            summed[k][b] = v.astype(bf16)

        @pl.loop(0, SLOTS, unroll=8)
        def _(o):
            zsend[k, o] = summed[k][chosen[o]]

        for d in (4, 3, 5, 2, 6, 1, 7):
            tz = lax.rem(z + d, NZ)
            sends.append(
                send(zsend.at[k, pl.ds(tz * NY, NY)], zrcv.at[k, z], zsnd.at[d, k], zrs.at[k], zdev(d))
            )
        zrcv[k, z] = zsend[k, pl.ds(z * NY, NY)]

    def wait_all(buf, k, sem):
        part = buf.at[pl.ds(0, 7)] if k is None else buf.at[k, pl.ds(0, 7)]
        pltpu.make_async_copy(part, part, sem if k is None else sem.at[k]).wait()

    def z_to_y(k):
        wait_all(zrcv, k, zrs)
        for d in (4, 3, 5, 2, 6, 1, 7):
            q = lax.rem(yc + d, NY)
            sends.append(send(zrcv.at[k, :, q], gbuf.at[k, :, yc], ysnd.at[d, k], yrs.at[k], ydev(d)))
        gbuf[k, :, yc] = zrcv[k, :, yc]

    def mul_right(k):
        wait_all(gbuf, k, yrs)
        if k == 0:
            load_f.wait()

        @pl.loop(0, 4)
        def _(i):
            part = gbuf[k, pl.ds(i * 2, 2)].reshape(256, W)
            wide = part.astype(f32)
            gsq[...] += jnp.sum((wide * wide).reshape(32, 8, W), axis=0)
            prod = jnp.dot(part, fac[1, pl.ds(k * W, W), :], preferred_element_type=f32)
            rows = pl.ds(pl.multiple_of(i * 256, 256), 256)
            if k > 0:
                prod = prod + acc[rows, :]
            if k == CH - 1:
                rp[rows, :] = prod.astype(bf16)
            else:
                acc[rows, :] = prod

    x1s, x2s = {}, {}
    x1s[0] = x1(0)
    x2s[0] = list(x2own(0))
    x1s[1] = x1(1)
    for t in range(CH + 4):
        if t < CH:
            x2s[t] += x2sum(t, x1s[t])
            if t + 1 < CH:
                x2s[t + 1] = list(x2own(t + 1))
            if t + 2 < CH:
                x1s[t + 2] = x1(t + 2)
        if 0 <= t - 1 < CH:
            pack_and_z(t - 1, x2s[t - 1])
        if 0 <= t - 3 < CH:
            z_to_y(t - 3)
        if 0 <= t - 4 < CH:
            mul_right(t - 4)

    def mul_left(j):
        @pl.loop(0, 4)
        def _(i):
            rows = pl.ds(pl.multiple_of(i * 256, 256), 256)
            prod = jnp.dot(fac[0, rows, :], rp[:, pl.ds(j * W, W)], preferred_element_type=f32)
            psq[...] += jnp.sum((prod * prod).reshape(32, 8, W), axis=0)
            pbuf[j, pl.ds(i * 2, 2)] = prod.astype(bf16).reshape(2, NY, ROWS, W)

        for d in (4, 3, 5, 2, 6, 1, 7):
            q = lax.rem(yc + d, NY)
            sends.append(send(pbuf.at[j, :, q], yrcv.at[j, yc], csnd.at[d, j], crs.at[j], ydev(d)))
        yrcv[j, yc] = pbuf[j, :, yc]

    def y_to_z(j):
        wait_all(yrcv, j, crs)
        for d in (4, 3, 5, 2, 6, 1, 7):
            tz = lax.rem(z + d, NZ)
            sends.append(send(yrcv.at[j, :, tz], fin[j].at[z], dsnd.at[d, j], drs.at[j], zdev(d)))
        fin[j][z] = yrcv[j, :, z]

    def exchange(buf, value, me, count, dev, row):
        buf[me] = value
        got = []
        for d in range(1, count):
            c = send(buf.at[me], buf.at[me], st_snd.at[row, d], st_rcv.at[row, d], dev(d))
            got.append(c)
        sends.extend(got)
        for c in got:
            c.wait_recv()

    for j in range(CH + 1):
        if j < CH:
            mul_left(j)
        if j > 0:
            y_to_z(j - 1)

    lane = lax.broadcasted_iota(jnp.int32, (8, 128), 1)
    sub = lax.broadcasted_iota(jnp.int32, (8, 128), 0)
    hot = ownmat[...] == lax.broadcasted_iota(jnp.int32, (PADB, 128), 1)
    used = jnp.sum(jnp.where(hot, 1.0, 0.0), axis=0, keepdims=True)
    gtot = jnp.sum(gsq[...], keepdims=True)
    ptot = jnp.sum(psq[...], keepdims=True)
    mine = jnp.where(sub == 0, gtot * used, jnp.where(sub == 1, ptot, 0.0))
    exchange(sty, jnp.where(lane == f, mine, 0.0), yc, NY, ydev, 0)
    exchange(stz, jnp.sum(sty[...], axis=0), z, NZ, zdev, 1)
    plane = jnp.sum(stz[...], axis=0)
    exchange(stx, plane, g, NX, xdev, 2)
    squares = jnp.sum(jnp.sum(stx[...], axis=0)[0:1, :], axis=1, keepdims=True)
    scale = 0.5 * math.sqrt(float(NX * GB * BS * BS)) / jnp.sqrt(squares)
    count = float(BS * BS)
    ratio = jnp.sqrt((plane[0:1, :] / count + small_eps) / (plane[1:2, :] / count + small_eps))
    per_block = jnp.sum(jnp.where(hot, scale * ratio, 0.0), axis=1, keepdims=True)
    sc[...] = jnp.broadcast_to(per_block, (PADB, W))
    bmax[...] = jnp.zeros_like(bmax)
    load_w.wait()

    for j in range(CH):
        wait_all(fin[j], None, drs.at[j])
        cols = pl.ds(j * W, W)

        @pl.loop(0, GB, unroll=4)
        def _(b):
            o = dkey[b]
            u = fin[j][lax.div(o, NY), lax.rem(o, NY)].astype(f32)
            upd = (sc[pl.ds(b, 1), :] * u).astype(bf16).astype(f32)
            nw = (win[b, :, cols].astype(f32) - learn_rate * upd).astype(bf16)
            out[b, :, cols] = nw
            mag = jnp.abs(nw.astype(f32))
            mag = jnp.maximum(mag[0:8], mag[8:16])
            m = bmax[b]
            for s in range(W // 128):
                m = jnp.maximum(m, mag[:, s * 128 : (s + 1) * 128])
            bmax[b] = m

    bid = lax.broadcasted_iota(jnp.int32, (GB, 8, 128), 0) + g * GB
    peak = bmax[...]
    tile = jnp.zeros((8, 128), f32)
    edges = (0, 64, 72, 80, 144)
    for t in range(4):
        inside = (bid >= edges[t]) & (bid < edges[t + 1])
        m = jnp.max(jnp.max(jnp.where(inside, peak, 0.0), axis=0), axis=0, keepdims=True)
        tile = jnp.where(sub == t, m, tile)
    exchange(mxy, tile, yc, NY, ydev, 3)
    exchange(mxz, jnp.max(mxy[...], axis=0), z, NZ, zdev, 4)
    exchange(mxx, jnp.max(mxz[...], axis=0), g, NX, xdev, 5)
    top = 1.0 / (jnp.max(jnp.max(mxx[...], axis=0), axis=1, keepdims=True) + small_eps)
    rid = lax.broadcasted_iota(jnp.int32, (PADB, W), 0) + g * GB
    inv = jnp.zeros((PADB, W), f32)
    for t in range(4):
        inside = (rid >= edges[t]) & (rid < edges[t + 1])
        inv = jnp.where(inside, top[t : t + 1, :], inv)
    sc[...] = inv

    @pl.loop(0, GB, unroll=2)
    def _(b):
        s = sc[pl.ds(b, 1), :]
        for c in range(CH):
            at = pl.ds(c * W, W)
            out[b, :, at] = (out[b, :, at].astype(f32) * s).astype(bf16)

    for c in sends:
        c.wait_send()


def per_device(grad_parts, factors, weights, block_owner):
    group = lax.axis_index("dp")
    owners = lax.dynamic_slice_in_dim(block_owner, group * GB, GB)
    ids = jnp.arange(GB, dtype=jnp.int32)
    slots = jnp.arange(SLOTS, dtype=jnp.int32)
    chosen = jnp.sum(jnp.where(owners[None, :] == slots[:, None], ids[None, :], 0), axis=1)
    padded = jnp.concatenate([owners, jnp.full((PADB - GB,), -1, jnp.int32)])
    ownmat = jnp.broadcast_to(padded[:, None], (PADB, 128))
    smem = pl.BlockSpec(memory_space=pltpu.SMEM)
    vmem = pl.BlockSpec(memory_space=pltpu.VMEM)
    hbm = pl.BlockSpec(memory_space=pl.ANY)
    dma = pltpu.SemaphoreType.DMA
    return pl.pallas_call(
        kernel,
        out_shape=jax.ShapeDtypeStruct((GB, ROWS, BS), bf16),
        in_specs=[smem, smem, vmem, hbm, hbm, hbm],
        out_specs=vmem,
        scratch_shapes=[
            pltpu.VMEM((CH, NX * GB, ROWS, W), bf16),
            pltpu.VMEM((2, BS, BS), bf16),
            pltpu.VMEM((GB, ROWS, BS), bf16),
            pltpu.VMEM((2, CH, HALF, ROWS, W), bf16),
            pltpu.VMEM((2, CH, HALF, ROWS, W), bf16),
            pltpu.VMEM((2, CH, GB, ROWS, W), bf16),
            [pltpu.VMEM((GB, ROWS, W), bf16)] * CH,
            pltpu.VMEM((CH, SLOTS, ROWS, W), bf16),
            pltpu.VMEM((CH, NZ, NY, ROWS, W), bf16),
            pltpu.VMEM((CH, NZ, NY, ROWS, W), bf16),
            pltpu.VMEM((BS, BS), f32),
            pltpu.VMEM((BS, BS), bf16),
            pltpu.VMEM((CH, NZ, NY, ROWS, W), bf16),
            pltpu.VMEM((CH, NY, NZ, ROWS, W), bf16),
            [pltpu.VMEM((NZ, NY, ROWS, W), bf16)] * CH,
            pltpu.VMEM((8, W), f32),
            pltpu.VMEM((8, W), f32),
            pltpu.VMEM((PADB, W), f32),
            pltpu.VMEM((GB, 8, 128), f32),
            pltpu.VMEM((NY, 8, 128), f32),
            pltpu.VMEM((NZ, 8, 128), f32),
            pltpu.VMEM((NX, 8, 128), f32),
            pltpu.VMEM((NY, 8, 128), f32),
            pltpu.VMEM((NZ, 8, 128), f32),
            pltpu.VMEM((NX, 8, 128), f32),
            dma((CH + 2,)),
            dma((3, 2, CH)),
            dma((3, 2, CH)),
            dma((8, CH)),
            dma((CH,)),
            dma((8, CH)),
            dma((CH,)),
            dma((8, CH)),
            dma((CH,)),
            dma((8, CH)),
            dma((CH,)),
            dma((6, 8)),
            dma((6, 8)),
        ],
        compiler_params=pltpu.CompilerParams(
            collective_id=0, has_side_effects=True, vmem_limit_bytes=56 * 2**20
        ),
        cost_estimate=pl.CostEstimate(flops=4 * BS**3, bytes_accessed=12 * 2**20, transcendentals=0),
        name="shampoo_step",
    )(chosen, owners, ownmat, grad_parts[0], factors.reshape(2, BS, BS), weights)


def solution(mesh):
    placed = (
        P("dp", None, "fsdp", None),
        P("dp", "fsdp", None, None, None, None),
        P("dp", "fsdp", None),
        P(),
    )
    return jax.shard_map(
        per_device, mesh=mesh, in_specs=placed, out_specs=P("dp", "fsdp", None), check_vma=False
    )
```

time: 365 us -> 163 us (0.45)
  blocking collectives: 210 us -> 0 us
  Pallas kernels: 0 us -> 159 us
  waiting for transfers between devices: 110 us -> 0 us
  between operations: 15.5 us -> 0.01 us
  other arithmetic: 10.4 us -> 0.66 us
  matrix products: 9.27 us -> 0 us
  starting transfers between devices: 6.11 us -> 0 us
    pallas_call x0 -> x1, Pallas kernels: none -> 159 us  [per_device(): pl.pallas_call(kernel, out_shape=jax.ShapeDtypeStruct((GB, ROWS, BS), bf1...]
    pmax x1 -> x0, blocking collectives: 75.2 us -> none  [per_device(): tensor_max = lax.pmax(local_peak, ('dp', 'fsdp'))]
    psum x1 -> x0, blocking collectives: 75.1 us -> none  [per_device(): squares_sum = lax.psum(jnp.sum(grad_squares), ('dp', 'fsdp'))]
    all_to_all x1 -> x0, blocking collectives: 60.1 us -> none  [per_device(): lax.all_to_all(outgoing, 'fsdp', split_axis=0, concat_axis=2, tiled=True)]
    reduce_scatter x1 -> x0, waiting for transfers between devices: 59.7 us -> none  [per_device(): lax.psum_scatter(grad_parts[0].astype(jnp.float32).astype(jnp.bfloat16),...]
    all_to_all x1 -> x0, waiting for transfers between devices: 49.6 us -> none  [per_device(): lax.all_to_all(update.reshape(slot_count, fsdp_count, shard_rows, block_s...]
    dot_general x1 -> x0, matrix products: 9.27 us -> none  [block_products(): jnp.dot(factor_pair[0], right_product, preferred_element_type=jnp.float32)]
    all_to_all x1 -> x0, starting transfers between devices: 6.11 us -> none  [per_device(): lax.all_to_all(update.reshape(slot_count, fsdp_count, shard_rows, block_s...]
  transfers between devices with their start and end apart: 2 -> 0, of which waited for: 2 -> 0; matrix products, arithmetic and copies ran while one was open for 0% -> 0% of each run, Pallas kernels for 0% -> 0%
where the time goes in v1:
time: 163 us
  Pallas kernels  159 us (98%)
  local copies, waits for them, and re-layouts  3.86 us (2%)
    pallas_call x1, Pallas kernels, per_device(): pl.pallas_call(kernel, out_shape=jax.ShapeDtypeStruct((GB, ROWS, BS), bf1...  159 us

profile of v1, /device:TPU:1, one launch (start us, length us, event | category | flops | bytes accessed | tf_op | source)
XLA Modules:
  0.0 163.2 jit_solution(5345673839275630236)
XLA Ops:
  0.0 0.8 dynamic_slice.3.dkey
  0.8 0.0 copy-start
  0.8 0.7 select_reduce_fusion.chosen
  1.4 0.7 broadcast_in_dim.23.ownmat
  2.1 0.0 copy-done
  2.1 158.7 %shampoo_step.1 = bf16[36,16,1024]{2,1,0:T(8,128)(2,1)} custom-call(s32[64]{0:T(128)} %select_reduce_fusion.chosen, s32[36]{0:T(128)} %copy-done, s32[40,128]{1,0:T(8,128)} %broadcast_in_dim.23.ownmat, bf16[144,16,1024]{2,1,0:T(8,128)(2,1)} %bitcast.2, bf16[2,1024,1024]{2,1,0:T(8,128)(2,1)} %bitcast.3, bf16[36,16,1024]{2,1,0:T(8,128)(2,1)} %weights.1), custom_call_target="tpu_custom_call" | custom-call | flops 4294967296 | bytes 12582912 | tf_op jit(solution)/shard_map/shampoo_step/pallas_call | solution.py:307
  160.8 2.4 %copy.6 = bf16[36,16,1024]{2,1,0:T(8,128)(2,1)} copy(bf16[36,16,1024]{2,1,0:T(8,128)(2,1)} %shampoo_step.1) | data formatting | bytes 2359296
  (1 shorter events, 0.0 us)
Async XLA Ops:
  0.8 1.3 copy-start

commit v2 on v1

v2 whole, which is shorter than its diff:
```python
import functools
import math

import jax
import jax.numpy as jnp
from jax import lax
from jax.experimental import pallas as pl
from jax.experimental.pallas import tpu as pltpu
from jax.sharding import PartitionSpec as P

BS = 1024
GB = 36
HALF = 18
NX, NZ, NY, NC = 4, 8, 4, 2
PAIRS = NZ * NY
SLOTS = PAIRS * NC
ROWS = 16
CH = 8
W = BS // CH
PADB = 40

learn_rate = 0.02
small_eps = 1e-06
f32 = jnp.float32
bf16 = jnp.bfloat16
MESH = pl.DeviceIdType.MESH


def kernel(
    owner, grads, factors, weights, out, inv_out,
    gin, fac, win, xa, xs, xb, summed, zsend, zrcv, gbuf, acc, rp, pbuf, yrcv, fin,
    gsq, psq, sc, bmax, sta, stb, mxa, mxb,
    ownmat, chosen_v, chosen, in_sem, xsnd, xrcv, zsnd, zrs, ysnd, yrs, csnd, crs, dsnd, drs,
    ea_snd, ea_rcv, eb_snd, eb_rcv,
):
    g = lax.axis_index("dp")
    f = lax.axis_index("fsdp")
    pair = lax.div(f, NC)
    core = lax.rem(f, NC)
    other = 1 - core

    def xdev(d):
        return {"dp": lax.rem(g + d, NX)}

    def xcdev(d):
        x = lax.rem(g + d // NC, NX)
        c = lax.rem(core + d % NC, NC)
        return {"dp": x, "fsdp": pair * NC + c}

    def pair_at(d):
        z = lax.rem(lax.div(pair, NY) + lax.div(d, NY), NZ)
        y = lax.rem(lax.rem(pair, NY) + lax.rem(d, NY), NY)
        return z * NY + y

    swap = {"fsdp": pair * NC + other}

    loads = [
        pltpu.make_async_copy(grads.at[:, :, pl.ds(k * W, W)], gin.at[k], in_sem.at[k])
        for k in range(CH)
    ]
    load_f = pltpu.make_async_copy(factors, fac, in_sem.at[CH])
    load_w = pltpu.make_async_copy(weights, win, in_sem.at[CH + 1])
    for c in loads:
        c.start()
    load_f.start()
    load_w.start()

    barrier = pltpu.get_barrier_semaphore()
    for d in range(1, NX * NC):
        pl.semaphore_signal(barrier, inc=1, device_id=xcdev(d), device_id_type=MESH)

    @pl.loop(1, PAIRS)
    def _(d):
        pl.semaphore_signal(
            barrier, inc=1, device_id={"fsdp": pair_at(d) * NC + core}, device_id_type=MESH
        )

    ownmat[...] = jnp.full((PADB, 128), -1, jnp.int32)
    for b in range(GB):
        ownmat[pl.ds(b, 1), :] = jnp.full((1, 128), owner[g * GB + b], jnp.int32)
    hot = ownmat[...] == lax.broadcasted_iota(jnp.int32, (PADB, 128), 1)
    picked = jnp.where(hot, lax.broadcasted_iota(jnp.int32, (PADB, 128), 0), 0)
    chosen_v[...] = jnp.broadcast_to(jnp.max(picked, axis=0, keepdims=True), (8, 128))
    load_c = pltpu.make_async_copy(chosen_v, chosen, in_sem.at[CH + 2])
    load_c.start()
    gsq[...] = jnp.zeros_like(gsq)
    psq[...] = jnp.zeros_like(psq)
    pl.semaphore_wait(barrier, NX * NC - 1 + PAIRS - 1)
    load_c.wait()

    sends = []

    def send(src, dst, ss, rs, dev):
        c = pltpu.make_async_remote_copy(
            src_ref=src, dst_ref=dst, send_sem=ss, recv_sem=rs, device_id=dev, device_id_type=MESH
        )
        c.start()
        return c

    gnext = lax.rem(g + 1, NX) * GB
    gprev = lax.rem(g + 3, NX) * GB
    gfar = lax.rem(g + 2, NX) * GB
    gown = g * GB

    def x1(k):
        loads[k].wait()
        a = send(gin.at[k, pl.ds(gfar, HALF)], xa.at[0, k], xsnd.at[0, 0, k], xrcv.at[0, 0, k], xdev(1))
        b = send(gin.at[k, pl.ds(gfar + HALF, HALF)], xa.at[1, k], xsnd.at[0, 1, k], xrcv.at[0, 1, k], xdev(3))
        sends.extend([a, b])
        return a, b

    def x2own(k):
        a = send(
            gin.at[k, pl.ds(gnext + HALF, HALF)], xb.at[0, k, pl.ds(HALF, HALF)],
            xsnd.at[1, 0, k], xrcv.at[1, 0, k], xdev(1),
        )
        b = send(
            gin.at[k, pl.ds(gprev, HALF)], xb.at[1, k, pl.ds(0, HALF)],
            xsnd.at[1, 1, k], xrcv.at[1, 1, k], xdev(3),
        )
        sends.extend([a, b])
        return a, b

    def x2sum(k, first):
        out_c = []
        for side, base in ((0, gnext), (1, gprev + HALF)):
            first[side].wait_recv()

            @pl.loop(0, HALF, unroll=3)
            def _(i):
                xs[side, k, i] = (gin[k, base + i].astype(f32) + xa[side, k, i].astype(f32)).astype(bf16)

            at = pl.ds(0, HALF) if side == 0 else pl.ds(HALF, HALF)
            out_c.append(
                send(
                    xs.at[side, k], xb.at[side, k, at],
                    xsnd.at[2, side, k], xrcv.at[2, side, k], xdev(1 if side == 0 else 3),
                )
            )
        sends.extend(out_c)
        return out_c

    def spread(src, dst, ss, rs):
        @pl.loop(1, PAIRS)
        def _(d):
            to = pair_at(d)
            send(src.at[to], dst.at[pair], ss, rs, {"fsdp": to * NC + core})

    def pack_and_z(k, got):
        for c in got:
            c.wait_recv()

        @pl.loop(0, GB, unroll=4)
        def _(b):
            v = gin[k, gown + b].astype(f32) + xb[0, k, b].astype(f32) + xb[1, k, b].astype(f32)
            summed[k][b] = v.astype(bf16)

        @pl.loop(0, PAIRS, unroll=4)
        def _(p):
            for c in range(NC):
                zsend[k, p, c] = summed[k][chosen[0, p * NC + c]]

        spread(zsend.at[k], zrcv.at[k], zsnd.at[k], zrs.at[k])
        zrcv[k, pair] = zsend[k, pair]

    def wait_all(buf, sem):
        part = buf.at[pl.ds(0, PAIRS - 1)]
        pltpu.make_async_copy(part, part, sem).wait()

    swaps = {}

    def z_to_y(k):
        wait_all(zrcv.at[k], zrs.at[k])
        swaps[k] = send(zrcv.at[k, :, other], gbuf.at[k, :, core], ysnd.at[k], yrs.at[k], swap)
        gbuf[k, :, core] = zrcv[k, :, core]

    def mul_right(k):
        swaps[k].wait()
        if k == 0:
            load_f.wait()

        @pl.loop(0, 4)
        def _(i):
            part = gbuf[k, pl.ds(i * 8, 8)].reshape(256, W)
            wide = part.astype(f32)
            gsq[...] += jnp.sum((wide * wide).reshape(32, 8, W), axis=0)
            prod = jnp.dot(part, fac[1, pl.ds(k * W, W), :], preferred_element_type=f32)
            rows = pl.ds(pl.multiple_of(i * 256, 256), 256)
            if k > 0:
                prod = prod + acc[rows, :]
            if k == CH - 1:
                rp[rows, :] = prod.astype(bf16)
            else:
                acc[rows, :] = prod

    x1s, x2s = {}, {}
    x1s[0] = x1(0)
    x2s[0] = list(x2own(0))
    x1s[1] = x1(1)
    for t in range(CH + 4):
        if t < CH:
            x2s[t] += x2sum(t, x1s[t])
            if t + 1 < CH:
                x2s[t + 1] = list(x2own(t + 1))
            if t + 2 < CH:
                x1s[t + 2] = x1(t + 2)
        if 0 <= t - 1 < CH:
            pack_and_z(t - 1, x2s[t - 1])
        if 0 <= t - 3 < CH:
            z_to_y(t - 3)
        if 0 <= t - 4 < CH:
            mul_right(t - 4)

    def mul_left(j):
        @pl.loop(0, 4)
        def _(i):
            rows = pl.ds(pl.multiple_of(i * 256, 256), 256)
            prod = jnp.dot(fac[0, rows, :], rp[:, pl.ds(j * W, W)], preferred_element_type=f32)
            psq[...] += jnp.sum((prod * prod).reshape(32, 8, W), axis=0)
            pbuf[j, pl.ds(i * 8, 8)] = prod.astype(bf16).reshape(8, NC, ROWS, W)

        spread(pbuf.at[j], yrcv.at[j], csnd.at[j], crs.at[j])
        yrcv[j, pair] = pbuf[j, pair]

    def y_to_z(j):
        wait_all(yrcv.at[j], crs.at[j])
        swaps[j] = send(yrcv.at[j, :, other], fin[j].at[:, core], dsnd.at[j], drs.at[j], swap)
        fin[j][:, core] = yrcv[j, :, core]

    def exchange(buf_a, buf_b, value, merge, row):
        me = g * NC + core
        buf_a[me] = value
        got = [
            send(buf_a.at[me], buf_a.at[me], ea_snd.at[row, d], ea_rcv.at[row, d], xcdev(d))
            for d in range(1, NX * NC)
        ]
        sends.extend(got)
        for c in got:
            c.wait_recv()
        buf_b[pair] = merge(buf_a[...])

        @pl.loop(1, PAIRS)
        def _(d):
            to = pair_at(d)
            send(buf_b.at[pair], buf_b.at[pair], eb_snd.at[row], eb_rcv.at[row], {"fsdp": to * NC + core})

        wait_all(buf_b, eb_rcv.at[row])

    for j in range(CH):
        mul_left(j)

    lane = lax.broadcasted_iota(jnp.int32, (8, 128), 1)
    sub = lax.broadcasted_iota(jnp.int32, (8, 128), 0)
    used = jnp.sum(jnp.where(hot, 1.0, 0.0), axis=0, keepdims=True)
    gtot = jnp.sum(gsq[...], keepdims=True)
    ptot = jnp.sum(psq[...], keepdims=True)
    mine = jnp.where(sub == 0, gtot * used, jnp.where(sub == 1, ptot, 0.0))
    lead = lax.broadcasted_iota(jnp.int32, (NX * NC, 8, 128), 0)

    def merge(t):
        plane = jnp.sum(jnp.where(lax.div(lead, NC) == g, t, 0.0), axis=0)
        return jnp.where(sub == 2, jnp.sum(t, axis=0)[0:1, :], plane)

    exchange(sta, stb, jnp.where(lane == f, mine, 0.0), merge, 0)
    for j in range(CH):
        y_to_z(j)
    plane = jnp.sum(stb[...], axis=0)
    squares = jnp.sum(plane[2:3, :], axis=1, keepdims=True)
    scale = 0.5 * math.sqrt(float(NX * GB * BS * BS)) / jnp.sqrt(squares)
    count = float(BS * BS)
    ratio = jnp.sqrt((plane[0:1, :] / count + small_eps) / (plane[1:2, :] / count + small_eps))
    per_block = jnp.sum(jnp.where(hot, scale * ratio, 0.0), axis=1, keepdims=True)
    sc[...] = jnp.broadcast_to(per_block, (PADB, W))
    bmax[...] = jnp.zeros_like(bmax)
    load_w.wait()

    for j in range(CH):
        swaps[j].wait_recv()
        cols = pl.ds(j * W, W)

        @pl.loop(0, GB, unroll=4)
        def _(b):
            o = owner[g * GB + b]
            u = fin[j][lax.div(o, NC), lax.rem(o, NC)].astype(f32)
            upd = (sc[pl.ds(b, 1), :] * u).astype(bf16).astype(f32)
            nw = (win[b, :, cols].astype(f32) - learn_rate * upd).astype(bf16)
            out[b, :, cols] = nw
            mag = jnp.abs(nw.astype(f32))
            mag = jnp.maximum(mag[0:8], mag[8:16])
            m = bmax[b]
            for s in range(W // 128):
                m = jnp.maximum(m, mag[:, s * 128 : (s + 1) * 128])
            bmax[b] = m

    bid = lax.broadcasted_iota(jnp.int32, (GB, 8, 128), 0) + g * GB
    peak = bmax[...]
    tile = jnp.zeros((8, 128), f32)
    edges = (0, 64, 72, 80, 144)
    for t in range(4):
        inside = (bid >= edges[t]) & (bid < edges[t + 1])
        m = jnp.max(jnp.max(jnp.where(inside, peak, 0.0), axis=0), axis=0, keepdims=True)
        tile = jnp.where(sub == t, m, tile)
    exchange(mxa, mxb, tile, lambda t: jnp.max(t, axis=0), 1)
    scale = 1.0 / (jnp.max(jnp.max(mxb[...], axis=0), axis=1, keepdims=True) + small_eps)
    rid = lax.broadcasted_iota(jnp.int32, (PADB, 128), 0) + g * GB
    inv = jnp.zeros((PADB, 128), f32)
    for t in range(4):
        inside = (rid >= edges[t]) & (rid < edges[t + 1])
        inv = jnp.where(inside, scale[t : t + 1, :], inv)
    inv_out[...] = inv

    for c in sends:
        c.wait_send()
    for k in range(CH):
        wait_all(zsend.at[k], zsnd.at[k])
        wait_all(pbuf.at[k], csnd.at[k])
        swaps[k].wait_send()
    for row, buf in ((0, stb), (1, mxb)):
        wait_all(buf, eb_snd.at[row])


def per_device(grad_parts, factors, weights, block_owner):
    smem = pl.BlockSpec(memory_space=pltpu.SMEM)
    vmem = pl.BlockSpec(memory_space=pltpu.VMEM)
    hbm = pl.BlockSpec(memory_space=pl.ANY)
    dma = pltpu.SemaphoreType.DMA
    new_weight, inv = pl.pallas_call(
        kernel,
        out_shape=(jax.ShapeDtypeStruct((GB, ROWS, BS), bf16), jax.ShapeDtypeStruct((PADB, 128), f32)),
        in_specs=[smem, hbm, hbm, hbm],
        out_specs=(vmem, vmem),
        scratch_shapes=[
            pltpu.VMEM((CH, NX * GB, ROWS, W), bf16),
            pltpu.VMEM((2, BS, BS), bf16),
            pltpu.VMEM((GB, ROWS, BS), bf16),
            pltpu.VMEM((2, CH, HALF, ROWS, W), bf16),
            pltpu.VMEM((2, CH, HALF, ROWS, W), bf16),
            pltpu.VMEM((2, CH, GB, ROWS, W), bf16),
            [pltpu.VMEM((GB, ROWS, W), bf16)] * CH,
            pltpu.VMEM((CH, PAIRS, NC, ROWS, W), bf16),
            pltpu.VMEM((CH, PAIRS, NC, ROWS, W), bf16),
            pltpu.VMEM((CH, PAIRS, NC, ROWS, W), bf16),
            pltpu.VMEM((BS, BS), f32),
            pltpu.VMEM((BS, BS), bf16),
            pltpu.VMEM((CH, PAIRS, NC, ROWS, W), bf16),
            pltpu.VMEM((CH, PAIRS, NC, ROWS, W), bf16),
            [pltpu.VMEM((PAIRS, NC, ROWS, W), bf16)] * CH,
            pltpu.VMEM((8, W), f32),
            pltpu.VMEM((8, W), f32),
            pltpu.VMEM((PADB, W), f32),
            pltpu.VMEM((GB, 8, 128), f32),
            pltpu.VMEM((NX * NC, 8, 128), f32),
            pltpu.VMEM((PAIRS, 8, 128), f32),
            pltpu.VMEM((NX * NC, 8, 128), f32),
            pltpu.VMEM((PAIRS, 8, 128), f32),
            pltpu.VMEM((PADB, 128), jnp.int32),
            pltpu.VMEM((8, 128), jnp.int32),
            pltpu.SMEM((8, 128), jnp.int32),
            dma((CH + 3,)),
            dma((3, 2, CH)),
            dma((3, 2, CH)),
            dma((CH,)),
            dma((CH,)),
            dma((CH,)),
            dma((CH,)),
            dma((CH,)),
            dma((CH,)),
            dma((CH,)),
            dma((CH,)),
            dma((2, 8)),
            dma((2, 8)),
            dma((2,)),
            dma((2,)),
        ],
        compiler_params=pltpu.CompilerParams(
            collective_id=0, has_side_effects=True, vmem_limit_bytes=56 * 2**20
        ),
        cost_estimate=pl.CostEstimate(flops=4 * BS**3, bytes_accessed=12 * 2**20, transcendentals=0),
        name="shampoo_step",
    )(block_owner, grad_parts[0], factors.reshape(2, BS, BS), weights)
    return (new_weight.astype(f32) * inv[:GB, :1, None]).astype(bf16)


def solution(mesh):
    placed = (
        P("dp", None, "fsdp", None),
        P("dp", "fsdp", None, None, None, None),
        P("dp", "fsdp", None),
        P(),
    )
    return jax.shard_map(
        per_device, mesh=mesh, in_specs=placed, out_specs=P("dp", "fsdp", None), check_vma=False
    )
```

time: 163 us -> 144 us (0.88)
  Pallas kernels: 159 us -> 141 us
  local copies, waits for them, and re-layouts: 3.86 us -> 0.84 us
  other arithmetic: 0.66 us -> 2.55 us
    pallas_call x1, Pallas kernels: 159 us -> 141 us  [per_device(): pl.pallas_call(kernel, out_shape=(jax.ShapeDtypeStruct((GB, ROWS, BS), bf...]
    convert_element_type x0 -> x1, other arithmetic: none -> 2.55 us  [per_device(): return (new_weight.astype(f32) * inv[:GB, :1, None]).astype(bf16)]
    unnamed x3 -> x0, local copies, waits for them, and re-layouts: 2.43 us -> none
where the time goes in v2:
time: 144 us
  Pallas kernels  141 us (98%)
  other arithmetic  2.55 us (2%)
    pallas_call x1, Pallas kernels, per_device(): pl.pallas_call(kernel, out_shape=(jax.ShapeDtypeStruct((GB, ROWS, BS), bf...  141 us

profile of v2, /device:TPU:1, one launch (start us, length us, event | category | flops | bytes accessed | tf_op | source)
XLA Modules:
  0.0 144.2 jit_solution(12769241931610372862)
XLA Ops:
  0.0 140.8 %shampoo_step.1 = (bf16[36,16,1024]{2,1,0:T(8,128)(2,1)}, f32[40,128]{1,0:T(8,128)}) custom-call(s32[144]{0:T(256)} %owner.1, bf16[144,16,1024]{2,1,0:T(8,128)(2,1)} %bitcast.2, bf16[2,1024,1024]{2,1,0:T(8,128)(2,1)} %bitcast.3, bf16[36,16,1024]{2,1,0:T(8,128)(2,1)} %weights.1), custom_call_target="tpu_custom_call" | custom-call | flops 4294967296 | bytes 12582912 | tf_op jit(solution)/shard_map/shampoo_step/pallas_call | solution.py:327
  140.8 0.8 slice_reduce_fusion
  141.6 2.5 %multiply_convert_fusion = bf16[36,16,1024]{2,1,0:T(8,128)(2,1)} fusion(bf16[36,16,1024]{2,1,0:T(8,128)(2,1)} %get-tuple-element.7, f32[36]{0:T(128)S(1)} %slice_reduce_fusion), kind=kLoop, calls=%fused_computation | loop fusion | flops 1769472 | bytes 2359440 | tf_op jit(solution)/shard_map/convert_element_type | solution.py:381

commit v3 on v2

--- a/solution.py
+++ b/solution.py
@@ -17,6 +17,8 @@
 ROWS = 16
 CH = 8
 W = BS // CH
+CJ = 4
+W2 = BS // CJ
 PADB = 40
 
 learn_rate = 0.02
@@ -141,9 +143,11 @@
         return out_c
 
     def spread(src, dst, ss, rs):
-        @pl.loop(1, PAIRS)
-        def _(d):
-            to = pair_at(d)
+        @pl.loop(0, PAIRS - 1)
+        def _(i):
+            n = lax.div(i, NY)
+            dz = NZ // 2 + (1 - 2 * lax.rem(n, 2)) * lax.div(n + 1, 2)
+            to = pair_at(dz * NY + NY - 1 - lax.rem(i, NY))
             send(src.at[to], dst.at[pair], ss, rs, {"fsdp": to * NC + core})
 
     def pack_and_z(k, got):
@@ -198,14 +202,14 @@
     x2s[0] = list(x2own(0))
     x1s[1] = x1(1)
     for t in range(CH + 4):
+        if 0 <= t - 1 < CH:
+            pack_and_z(t - 1, x2s[t - 1])
         if t < CH:
             x2s[t] += x2sum(t, x1s[t])
             if t + 1 < CH:
                 x2s[t + 1] = list(x2own(t + 1))
             if t + 2 < CH:
                 x1s[t + 2] = x1(t + 2)
-        if 0 <= t - 1 < CH:
-            pack_and_z(t - 1, x2s[t - 1])
         if 0 <= t - 3 < CH:
             z_to_y(t - 3)
         if 0 <= t - 4 < CH:
@@ -215,9 +219,9 @@
         @pl.loop(0, 4)
         def _(i):
             rows = pl.ds(pl.multiple_of(i * 256, 256), 256)
-            prod = jnp.dot(fac[0, rows, :], rp[:, pl.ds(j * W, W)], preferred_element_type=f32)
-            psq[...] += jnp.sum((prod * prod).reshape(32, 8, W), axis=0)
-            pbuf[j, pl.ds(i * 8, 8)] = prod.astype(bf16).reshape(8, NC, ROWS, W)
+            prod = jnp.dot(fac[0, rows, :], rp[:, pl.ds(j * W2, W2)], preferred_element_type=f32)
+            psq[...] += jnp.sum((prod * prod).reshape(32, 8, W2), axis=0)
+            pbuf[j, pl.ds(i * 8, 8)] = prod.astype(bf16).reshape(8, NC, ROWS, W2)
 
         spread(pbuf.at[j], yrcv.at[j], csnd.at[j], crs.at[j])
         yrcv[j, pair] = pbuf[j, pair]
@@ -246,7 +250,7 @@
 
         wait_all(buf_b, eb_rcv.at[row])
 
-    for j in range(CH):
+    for j in range(CJ):
         mul_left(j)
 
     lane = lax.broadcasted_iota(jnp.int32, (8, 128), 1)
@@ -262,7 +266,7 @@
         return jnp.where(sub == 2, jnp.sum(t, axis=0)[0:1, :], plane)
 
     exchange(sta, stb, jnp.where(lane == f, mine, 0.0), merge, 0)
-    for j in range(CH):
+    for j in range(CJ):
         y_to_z(j)
     plane = jnp.sum(stb[...], axis=0)
     squares = jnp.sum(plane[2:3, :], axis=1, keepdims=True)
@@ -270,13 +274,13 @@
     count = float(BS * BS)
     ratio = jnp.sqrt((plane[0:1, :] / count + small_eps) / (plane[1:2, :] / count + small_eps))
     per_block = jnp.sum(jnp.where(hot, scale * ratio, 0.0), axis=1, keepdims=True)
-    sc[...] = jnp.broadcast_to(per_block, (PADB, W))
+    sc[...] = jnp.broadcast_to(per_block, (PADB, W2))
     bmax[...] = jnp.zeros_like(bmax)
     load_w.wait()
 
-    for j in range(CH):
+    for j in range(CJ):
         swaps[j].wait_recv()
-        cols = pl.ds(j * W, W)
+        cols = pl.ds(j * W2, W2)
 
         @pl.loop(0, GB, unroll=4)
         def _(b):
@@ -288,7 +292,7 @@
             mag = jnp.abs(nw.astype(f32))
             mag = jnp.maximum(mag[0:8], mag[8:16])
             m = bmax[b]
-            for s in range(W // 128):
+            for s in range(W2 // 128):
                 m = jnp.maximum(m, mag[:, s * 128 : (s + 1) * 128])
             bmax[b] = m
 
@@ -313,10 +317,20 @@
         c.wait_send()
     for k in range(CH):
         wait_all(zsend.at[k], zsnd.at[k])
+    for k in range(CJ):
         wait_all(pbuf.at[k], csnd.at[k])
         swaps[k].wait_send()
     for row, buf in ((0, stb), (1, mxb)):
         wait_all(buf, eb_snd.at[row])
+
+
+def rescale(weight, inv, out):
+    @pl.loop(0, GB, unroll=4)
+    def _(b):
+        s = inv[pl.ds(b, 1), :]
+        for c in range(BS // 128):
+            at = pl.ds(c * 128, 128)
+            out[b, :, at] = (weight[b, :, at].astype(f32) * s).astype(bf16)
 
 
 def per_device(grad_parts, factors, weights, block_owner):
@@ -342,12 +356,12 @@
             pltpu.VMEM((CH, PAIRS, NC, ROWS, W), bf16),
             pltpu.VMEM((BS, BS), f32),
             pltpu.VMEM((BS, BS), bf16),
-            pltpu.VMEM((CH, PAIRS, NC, ROWS, W), bf16),
-            pltpu.VMEM((CH, PAIRS, NC, ROWS, W), bf16),
-            [pltpu.VMEM((PAIRS, NC, ROWS, W), bf16)] * CH,
+            pltpu.VMEM((CJ, PAIRS, NC, ROWS, W2), bf16),
+            pltpu.VMEM((CJ, PAIRS, NC, ROWS, W2), bf16),
+            [pltpu.VMEM((PAIRS, NC, ROWS, W2), bf16)] * CJ,
             pltpu.VMEM((8, W), f32),
-            pltpu.VMEM((8, W), f32),
-            pltpu.VMEM((PADB, W), f32),
+            pltpu.VMEM((8, W2), f32),
+            pltpu.VMEM((PADB, W2), f32),
             pltpu.VMEM((GB, 8, 128), f32),
             pltpu.VMEM((NX * NC, 8, 128), f32),
             pltpu.VMEM((PAIRS, 8, 128), f32),
@@ -378,7 +392,14 @@
         cost_estimate=pl.CostEstimate(flops=4 * BS**3, bytes_accessed=12 * 2**20, transcendentals=0),
         name="shampoo_step",
     )(block_owner, grad_parts[0], factors.reshape(2, BS, BS), weights)
-    return (new_weight.astype(f32) * inv[:GB, :1, None]).astype(bf16)
+    return pl.pallas_call(
+        rescale,
+        out_shape=jax.ShapeDtypeStruct((GB, ROWS, BS), bf16),
+        in_specs=[vmem, vmem],
+        out_specs=vmem,
+        cost_estimate=pl.CostEstimate(flops=GB * ROWS * BS, bytes_accessed=3 * 2**20, transcendentals=0),
+        name="rescale",
+    )(new_weight, inv)
 
 
 def solution(mesh):

time: 144 us -> 141 us (0.979)
  other arithmetic: 2.55 us -> 0 us
    convert_element_type x1 -> x0, other arithmetic: 2.55 us -> none  [per_device(): return (new_weight.astype(f32) * inv[:GB, :1, None]).astype(bf16)]
    pallas_call x0 -> x1, Pallas kernels: none -> 2.55 us  [per_device(): pl.pallas_call(rescale, out_shape=jax.ShapeDtypeStruct((GB, ROWS, BS), bf...]
    pallas_call x1, Pallas kernels: 141 us -> 139 us  [per_device(): pl.pallas_call(kernel, out_shape=(jax.ShapeDtypeStruct((GB, ROWS, BS), bf...]
where the time goes in v3:
time: 141 us
  Pallas kernels  141 us (100%)
    pallas_call x1, Pallas kernels, per_device(): pl.pallas_call(kernel, out_shape=(jax.ShapeDtypeStruct((GB, ROWS, BS), bf...  139 us

profile of v3, /device:TPU:1, one launch (start us, length us, event | category | flops | bytes accessed | tf_op | source)
XLA Modules:
  0.0 141.3 jit_solution(12040384587100526781)
XLA Ops:
  0.0 138.7 %shampoo_step.1 = (bf16[36,16,1024]{2,1,0:T(8,128)(2,1)}, f32[40,128]{1,0:T(8,128)}) custom-call(s32[144]{0:T(256)} %owner.1, bf16[144,16,1024]{2,1,0:T(8,128)(2,1)} %bitcast.2, bf16[2,1024,1024]{2,1,0:T(8,128)(2,1)} %bitcast.3, bf16[36,16,1024]{2,1,0:T(8,128)(2,1)} %weights.1), custom_call_target="tpu_custom_call" | custom-call | flops 4294967296 | bytes 12582912 | tf_op jit(solution)/shard_map/shampoo_step/pallas_call | solution.py:341
  138.8 2.5 %rescale.1 = bf16[36,16,1024]{2,1,0:T(8,128)(2,1)} custom-call(bf16[36,16,1024]{2,1,0:T(8,128)(2,1)} %get-tuple-element.7.weight, f32[40,128]{1,0:T(8,128)} %get-tuple-element.8.inv), custom_call_target="tpu_custom_call" | custom-call | flops 589824 | bytes 3145728 | tf_op jit(solution)/shard_map/rescale/pallas_call | solution.py:395

commit v4 on v3

--- a/solution.py
+++ b/solution.py
@@ -32,7 +32,7 @@
     owner, grads, factors, weights, out, inv_out,
     gin, fac, win, xa, xs, xb, summed, zsend, zrcv, gbuf, acc, rp, pbuf, yrcv, fin,
     gsq, psq, sc, bmax, sta, stb, mxa, mxb,
-    ownmat, chosen_v, chosen, in_sem, xsnd, xrcv, zsnd, zrs, ysnd, yrs, csnd, crs, dsnd, drs,
+    ownmat, chosen_v, chosen, fresh, in_sem, xsnd, xrcv, zsnd, zrs, ysnd, yrs, csnd, crs, dsnd, drs,
     ea_snd, ea_rcv, eb_snd, eb_rcv,
 ):
     g = lax.axis_index("dp")
@@ -201,7 +201,7 @@
     x1s[0] = x1(0)
     x2s[0] = list(x2own(0))
     x1s[1] = x1(1)
-    for t in range(CH + 4):
+    for t in range(CH + 5):
         if 0 <= t - 1 < CH:
             pack_and_z(t - 1, x2s[t - 1])
         if t < CH:
@@ -210,20 +210,31 @@
                 x2s[t + 1] = list(x2own(t + 1))
             if t + 2 < CH:
                 x1s[t + 2] = x1(t + 2)
-        if 0 <= t - 3 < CH:
-            z_to_y(t - 3)
         if 0 <= t - 4 < CH:
-            mul_right(t - 4)
+            z_to_y(t - 4)
+        if 0 <= t - 5 < CH:
+            mul_right(t - 5)
 
     def mul_left(j):
         @pl.loop(0, 4)
         def _(i):
-            rows = pl.ds(pl.multiple_of(i * 256, 256), 256)
+            turn = lax.rem(i + lax.div(pair, 8) + 2, 4)
+            rows = pl.ds(pl.multiple_of(turn * 256, 256), 256)
             prod = jnp.dot(fac[0, rows, :], rp[:, pl.ds(j * W2, W2)], preferred_element_type=f32)
             psq[...] += jnp.sum((prod * prod).reshape(32, 8, W2), axis=0)
-            pbuf[j, pl.ds(i * 8, 8)] = prod.astype(bf16).reshape(8, NC, ROWS, W2)
-
-        spread(pbuf.at[j], yrcv.at[j], csnd.at[j], crs.at[j])
+            pbuf[j, pl.ds(turn * 8, 8)] = prod.astype(bf16).reshape(8, NC, ROWS, W2)
+            if j == 0:
+
+                @pl.loop(0, 8)
+                def _(n):
+                    to = turn * 8 + lax.rem(n + pair, 8)
+
+                    @pl.when(to != pair)
+                    def _():
+                        send(pbuf.at[j, to], yrcv.at[j, pair], csnd.at[j], crs.at[j], {"fsdp": to * NC + core})
+
+        if j > 0:
+            spread(pbuf.at[j], yrcv.at[j], csnd.at[j], crs.at[j])
         yrcv[j, pair] = pbuf[j, pair]
 
     def y_to_z(j):
@@ -278,6 +289,7 @@
     bmax[...] = jnp.zeros_like(bmax)
     load_w.wait()
 
+    stores = []
     for j in range(CJ):
         swaps[j].wait_recv()
         cols = pl.ds(j * W2, W2)
@@ -288,13 +300,16 @@
             u = fin[j][lax.div(o, NC), lax.rem(o, NC)].astype(f32)
             upd = (sc[pl.ds(b, 1), :] * u).astype(bf16).astype(f32)
             nw = (win[b, :, cols].astype(f32) - learn_rate * upd).astype(bf16)
-            out[b, :, cols] = nw
+            fresh[b, :, cols] = nw
             mag = jnp.abs(nw.astype(f32))
             mag = jnp.maximum(mag[0:8], mag[8:16])
             m = bmax[b]
             for s in range(W2 // 128):
                 m = jnp.maximum(m, mag[:, s * 128 : (s + 1) * 128])
             bmax[b] = m
+
+        stores.append(pltpu.make_async_copy(fresh.at[:, :, cols], out.at[:, :, cols], in_sem.at[CH + 3 + j]))
+        stores[j].start()
 
     bid = lax.broadcasted_iota(jnp.int32, (GB, 8, 128), 0) + g * GB
     peak = bmax[...]
@@ -312,6 +327,8 @@
         inside = (rid >= edges[t]) & (rid < edges[t + 1])
         inv = jnp.where(inside, scale[t : t + 1, :], inv)
     inv_out[...] = inv
+    for c in stores:
+        c.wait()
 
     for c in sends:
         c.wait_send()
@@ -342,7 +359,7 @@
         kernel,
         out_shape=(jax.ShapeDtypeStruct((GB, ROWS, BS), bf16), jax.ShapeDtypeStruct((PADB, 128), f32)),
         in_specs=[smem, hbm, hbm, hbm],
-        out_specs=(vmem, vmem),
+        out_specs=(hbm, vmem),
         scratch_shapes=[
             pltpu.VMEM((CH, NX * GB, ROWS, W), bf16),
             pltpu.VMEM((2, BS, BS), bf16),
@@ -370,7 +387,8 @@
             pltpu.VMEM((PADB, 128), jnp.int32),
             pltpu.VMEM((8, 128), jnp.int32),
             pltpu.SMEM((8, 128), jnp.int32),
-            dma((CH + 3,)),
+            pltpu.VMEM((GB, ROWS, BS), bf16),
+            dma((CH + 3 + CJ,)),
             dma((3, 2, CH)),
             dma((3, 2, CH)),
             dma((CH,)),

time: 141 us -> 140 us (level)
  no operation moved by 1% of the time
where the time goes in v4:
time: 140 us
  Pallas kernels  140 us (100%)
    pallas_call x1, Pallas kernels, per_device(): pl.pallas_call(kernel, out_shape=(jax.ShapeDtypeStruct((GB, ROWS, BS), bf...  138 us

profile of v4, /device:TPU:1, one launch (start us, length us, event | category | flops | bytes accessed | tf_op | source)
XLA Modules:
  0.0 140.1 jit_solution(13068508980972643990)
XLA Ops:
  0.0 137.5 %shampoo_step.1 = (bf16[36,16,1024]{2,1,0:T(8,128)(2,1)}, f32[40,128]{1,0:T(8,128)}) custom-call(s32[144]{0:T(256)} %owner.1, bf16[144,16,1024]{2,1,0:T(8,128)(2,1)} %bitcast.2, bf16[2,1024,1024]{2,1,0:T(8,128)(2,1)} %bitcast.3, bf16[36,16,1024]{2,1,0:T(8,128)(2,1)} %weights.1), custom_call_target="tpu_custom_call" | custom-call | flops 4294967296 | bytes 12582912 | tf_op jit(solution)/shard_map/shampoo_step/pallas_call | solution.py:358
  137.6 2.5 %rescale.1 = bf16[36,16,1024]{2,1,0:T(8,128)(2,1)} custom-call(bf16[36,16,1024]{2,1,0:T(8,128)(2,1)} %get-tuple-element.7.weight, f32[40,128]{1,0:T(8,128)} %get-tuple-element.8.inv), custom_call_target="tpu_custom_call" | custom-call | flops 589824 | bytes 3145728 | tf_op jit(solution)/shard_map/rescale/pallas_call | solution.py:413
